TPU v7x, 32 devices: a whole 2x2x4 slice. The times are simulated.
32 devices in a mesh: img: 2 (over x), atom: 16 (over z, y, core).
Axes of the slice: x: 2, y: 2, z: 4, core: 2. Of those that a mesh axis runs over, the one named last changes fastest.
Arguments:
- density: bfloat16 [2, 9, 9, 49152], P('img', None, None, 'atom'), may hold values from -1.5 to 1.5
- energy_density: bfloat16 [2, 9, 9, 49152], P('img', None, None, 'atom'), may hold values from -1.5 to 1.5
- dham: bfloat16 [2, 3, 9, 9, 49152], P('img', None, None, None, 'atom'), may hold values from -1.5 to 1.5
- dovl: bfloat16 [2, 3, 9, 9, 49152], P('img', None, None, None, 'atom'), may hold values from -1.5 to 1.5
- pair_owner: int32 [2, 49152], P('img', 'atom'), may hold values from 0 to 511
- pair_partner: int32 [2, 49152], P('img', 'atom'), may hold values from 0 to 8191, as said below
- partner_species: int32 [2, 49152], P('img', 'atom'), may hold values from 0 to 3, as said below
- pair_count: int32 [2, 16], P('img', 'atom'), may hold values from 768 to 3072, as said below
- species: int32 [8192], P('atom'), may hold values from 0 to 3
- orbitals: int32 [4], replicated, may hold values from 1 to 9, as said below
- coords: float32 [2, 3, 8192], P('img', None, 'atom')
- reactant: float32 [3, 8192], P(None, 'atom')
- product: float32 [3, 8192], P(None, 'atom')
Outputs:
- band_force: float32 [2, 3, 8192], P('img', None, 'atom')
- tangent_force: float32 [2], P('img')
Inputs may be any that keep to these rules, and one draw needn't show every extreme that they name: `pair_count`: each owner's live slots are its first ones; in every image some owner has all 3072 slots live, and every owner at least a quarter of them. partner_species[i, p] equals species[pair_partner[i, p]]. `pair_partner`: partners may be any atoms of the image; the first slot of owner o has its partner among the atoms of owner (o + 8) modulo 16 (owner o holds atoms o * 512 to o * 512 + 511). Species 0 has all 9 orbitals and the last species one.
All inputs are finite; a program needn't handle non-finite values.
Results may differ from a plain program's by a relative error of at most 0.0003.
Values sent between devices are 32-bit elements; how exact they have to be, the bound alone decides.
A program may use at most 64 MiB of HBM per device.

v0:
```python
import jax
import jax.numpy as jnp
from jax import lax
from jax.sharding import PartitionSpec as P

spring_const = 1.0
tangent_eps = 1e-06


def passed_along(block, axis, distance):
    devices = range(lax.axis_size(axis))
    route = [(i - distance, i) for i in devices if i - distance in devices]
    return lax.ppermute(block, axis, route)


def local(
    density,
    energy_density,
    dham,
    dovl,
    pair_owner,
    pair_partner,
    partner_species,
    pair_count,
    species,
    orbitals,
    coords,
    reactant,
    product,
):
    n_slots = density.shape[-1]
    n_orbit = density.shape[1]
    atoms_local = species.shape[0]
    total_atoms = atoms_local * lax.axis_size("atom")
    current = coords[0]
    before = passed_along(current, "img", 1)
    after = passed_along(current, "img", -1)
    first_image = lax.axis_index("img") == 0
    final_image = lax.axis_index("img") == lax.axis_size("img") - 1
    before = jnp.where(first_image, reactant, before)
    after = jnp.where(final_image, product, after)
    tangent = after - before
    ahead_part = jnp.sum((after - current) ** 2)
    behind_part = jnp.sum((current - before) ** 2)
    length_part = jnp.sum(tangent * tangent)
    ahead, behind, length = lax.psum((ahead_part, behind_part, length_part), "atom")
    unit = tangent / jnp.sqrt(length + tangent_eps)
    slots = jnp.arange(n_slots, dtype=jnp.int32)
    live = slots < pair_count[0, 0]
    owner_local = pair_owner[0]
    own_species = jnp.take(species, owner_local, axis=0)
    kinds = jnp.arange(orbitals.shape[0], dtype=jnp.int32)
    own_orbitals = jnp.sum(
        jnp.where(kinds[:, None] == own_species[None, :], orbitals[:, None], 0), axis=0
    )
    partner_orbitals = jnp.sum(
        jnp.where(kinds[:, None] == partner_species[0][None, :], orbitals[:, None], 0), axis=0
    )
    levels = jnp.arange(n_orbit, dtype=jnp.int32)
    row_ok = (levels[:, None] < own_orbitals[None, :]) & live[None, :]
    col_ok = levels[:, None] < partner_orbitals[None, :]
    mask = (row_ok[:, None, :] & col_ok[None, :, :]).astype(jnp.bfloat16)
    masked_density = density[0] * mask
    masked_energy = energy_density[0] * mask
    term_ham = jnp.einsum(
        "abp,cabp->cp", masked_density, dham[0], preferred_element_type=jnp.float32
    )
    term_ovl = jnp.einsum(
        "abp,cabp->cp", masked_energy, dovl[0], preferred_element_type=jnp.float32
    )
    pair_force = -2.0 * (term_ham - term_ovl)
    my_index = lax.axis_index("atom")
    owner_atom = my_index * atoms_local + owner_local
    partial_value = jnp.zeros((3, total_atoms), jnp.float32)
    partial_value = partial_value.at[:, owner_atom].add(pair_force)
    partial_value = partial_value.at[:, pair_partner[0]].add(-pair_force)
    force = lax.psum_scatter(partial_value, "atom", scatter_dimension=1, tiled=True)
    tangent_force = lax.psum(jnp.sum(force * unit), "atom")
    spring = spring_const * (jnp.sqrt(ahead) - jnp.sqrt(behind))
    band_force = force - tangent_force * unit + spring * unit
    return (band_force[None], jnp.reshape(tangent_force, (1,)))


def solution(mesh):
    return jax.shard_map(
        local,
        mesh=mesh,
        in_specs=(
            P("img", None, None, "atom"),
            P("img", None, None, "atom"),
            P("img", None, None, None, "atom"),
            P("img", None, None, None, "atom"),
            P("img", "atom"),
            P("img", "atom"),
            P("img", "atom"),
            P("img", "atom"),
            P("atom"),
            P(),
            P("img", None, "atom"),
            P(None, "atom"),
            P(None, "atom"),
        ),
        out_specs=(P("img", None, "atom"), P("img")),
        check_vma=False,
    )
```

profile of v0, /device:TPU:0, one launch (start us, length us, event | category | flops | bytes accessed | tf_op | source)
XLA Modules:
  0.0 197.0 jit_solution(10861787347791936784)
XLA Ops:
  7.2 0.7 copy.57
  7.9 1.3 collective-permute-start
  9.2 4.8 %collective-permute-start.1 = (f32[3,512]{1,0:T(4,128)S(1)}, f32[3,512]{1,0:T(4,128)S(1)}, u32[]{:S(2)}, u32[]{:S(2)}) collective-permute-start(f32[3,512]{1,0:T(4,128)S(1)} %bitcast.56), channel_id=1, source_target_pairs={{0,16},{1,17},{2,18},{3,19},{4,20},{5,21},{6,22},{7,23},{8,24},{9,... | collective-permute-start | bytes 18440 | tf_op jit(solution)/shard_map/ppermute | solution.py:13
  14.1 0.7 compare_select_fusion.1
  14.9 19.5 %gather_fusion = s32[3072]{0:T(1024)S(1)} fusion(s32[512]{0:T(512)S(1)} %copy-done, s32[3072]{0:T(1024)S(1)} %broadcast_clamp_fusion), kind=kCustom, calls=%fused_computation | custom fusion | bytes 36864 | tf_op jit(solution)/shard_map/jit(_take)/gather | solution.py:51
  35.2 0.1 select_reduce_fusion.1
  35.4 0.5 fusion.7
  36.0 1.0 copy-done.1
  37.0 1.1 multiply_reduce_fusion.1
  38.1 0.4 copy-done.2
  38.5 1.2 multiply_reduce_fusion
  39.7 0.5 copy.38
  40.2 0.5 copy.46
  40.7 19.2 %scatter_custom_fusion = f32[3,8192]{0,1:T(8,128)} fusion(s32[3072]{0:T(1024)S(1)} %bitcast.54, f32[]{:T(128)} %constant.13.clone.1, f32[3072,3]{1,0:T(8,128)S(1)} %copy.38, f32[3072,3]{1,0:T(8,128)S(1)} %copy.46, f32[]{:T(128)} %constant.37.clone.1), kind=kCustom, calls=%fused_computation.7 | custom fusion | flops 27648 | bytes 3244040 | tf_op jit(solution)/shard_map/scatter-add | solution.py:75
  59.9 21.1 %scatter_custom_fusion.1 = f32[3,8192]{0,1:T(8,128)} fusion(f32[3,8192]{0,1:T(8,128)} %scatter_custom_fusion, s32[3072]{0:T(1024)S(1)} %bitcast.52, f32[3072,3]{1,0:T(8,128)S(1)} %copy.38, f32[3072,3]{1,0:T(8,128)S(1)} %copy.46, f32[]{:T(128)} %constant.37.clone.1), kind=kCustom, calls=%fused_computation.9 | custom fusion | flops 36864 | bytes 3244544 | tf_op jit(solution)/shard_map/scatter-add | solution.py:76
  81.0 0.6 copy-done.6
  81.7 0.6 multiply_reduce_fusion.5
  82.3 34.9 %psum.28 = f32[]{:T(128)} all-reduce(f32[]{:T(128)} %get-tuple-element.19), channel_id=1, replica_groups=mesh['img'=2,'atom'=16] {'atom'}, use_global_device_ids=true, to_apply=%region_6.7 | all-reduce | flops 1 | bytes 8 | tf_op jit(solution)/shard_map/psum | solution.py:46
  117.9 37.2 %reduce-scatter.4.cloned.1.call-done = f32[512,3]{1,0:T(8,128)} async-done(((f32[8192,3]{1,0:T(8,128)}), f32[512,3]{1,0:T(8,128)}) %reduce-scatter.4.cloned.1.call-update) | async-done | bytes 6160
  155.1 1.1 copy.48
  156.1 0.6 multiply_reduce_fusion.4
  156.7 30.8 %all-reduce = (f32[]{:T(128)}, f32[]{:T(128)}, f32[]{:T(128)}) all-reduce(f32[]{:T(128)} %get-tuple-element.23, f32[]{:T(128)} %get-tuple-element.24, f32[]{:T(128)} %multiply_reduce_fusion.4), channel_id=1, replica_groups=mesh['img'=2,'atom'=16] {'atom'}, use_global_device_ids=true, to_apply=%region_10.11 | all-reduce | flops 3 | bytes 24 | tf_op jit(solution)/shard_map/psum | solution.py:46
  188.9 0.7 add_bitcast_fusion
  189.6 0.6 copy.30
  (30 shorter events, 0.3 us)
Async XLA Ops:
  7.2 7.7 %copy-start = (s32[512]{0:T(512)S(1)}, s32[512]{0:T(512)}, u32[]{:S(2)}) copy-start(s32[512]{0:T(512)} %param.21) | copy-start | bytes 6148
  7.2 147.9 %reduce-scatter.4.cloned.1.call-start = ((), (), s32[]{:S(2)}) async-start(), calls=%async_computation.1 | async-start | bytes 4456448
  7.9 73.1 %collective-permute-start = (f32[3,512]{1,0:T(4,128)S(1)}, f32[3,512]{1,0:T(4,128)S(1)}, u32[]{:S(2)}, u32[]{:S(2)}) collective-permute-start(f32[3,512]{1,0:T(4,128)S(1)} %bitcast.55), channel_id=1, source_target_pairs={{16,0},{17,1},{18,2},{19,3},{20,4},{21,5},{22,6},{23,7},{24,8},{25... | collective-permute-start | bytes 18440 | tf_op jit(solution)/shard_map/ppermute | solution.py:13
  9.2 71.8 %collective-permute-start.1 = (f32[3,512]{1,0:T(4,128)S(1)}, f32[3,512]{1,0:T(4,128)S(1)}, u32[]{:S(2)}, u32[]{:S(2)}) collective-permute-start(f32[3,512]{1,0:T(4,128)S(1)} %bitcast.56), channel_id=1, source_target_pairs={{0,16},{1,17},{2,18},{3,19},{4,20},{5,21},{6,22},{7,23},{8,24},{9,... | collective-permute-start | bytes 18440 | tf_op jit(solution)/shard_map/ppermute | solution.py:13
  14.8 19.6 %copy-start.5 = (s32[1,3072]{1,0:T(1,128)S(1)}, s32[1,3072]{1,0:T(1,128)}, u32[]{:S(2)}) copy-start(s32[1,3072]{1,0:T(1,128)} %param.17) | copy-start | bytes 36868
  14.8 20.3 %copy-start.7 = (s32[1,3072]{1,0:T(1,128)S(1)}, s32[1,3072]{1,0:T(1,128)}, u32[]{:S(2)}) copy-start(s32[1,3072]{1,0:T(1,128)} %param.18) | copy-start | bytes 36868
  14.8 20.3 %copy-start.8 = (s32[1,3072]{1,0:T(1,128)S(1)}, s32[1,3072]{1,0:T(1,128)}, u32[]{:S(2)}) copy-start(s32[1,3072]{1,0:T(1,128)} %param.19) | copy-start | bytes 36868
  14.9 20.3 %copy-start.11 = (s32[4]{0:T(128)S(1)}, s32[4]{0:T(128)}, u32[]{:S(2)}) copy-start(s32[4]{0:T(128)} %param.22) | copy-start | bytes 52
  14.9 20.5 %copy-start.3 = (bf16[1,9,9,3072]{3,2,1,0:T(8,128)(2,1)S(1)}, bf16[1,9,9,3072]{3,2,1,0:T(8,128)(2,1)}, u32[]{:S(2)}) copy-start(bf16[1,9,9,3072]{3,2,1,0:T(8,128)(2,1)} %param.14) | copy-start | bytes 1492996
  14.9 20.5 %copy-start.4 = (bf16[1,9,9,3072]{3,2,1,0:T(8,128)(2,1)S(1)}, bf16[1,9,9,3072]{3,2,1,0:T(8,128)(2,1)}, u32[]{:S(2)}) copy-start(bf16[1,9,9,3072]{3,2,1,0:T(8,128)(2,1)} %param.13) | copy-start | bytes 1492996
  35.4 1.6 copy-start.1
  37.0 1.6 copy-start.2
  80.9 0.7 copy-start.6
  80.9 0.7 copy-start.9
  80.9 0.7 copy-start.10
Sparse Core Ops, SparseCore 0:
  81.1 73.9 reduce-scatter.3
where the time goes:
time: 198 us; the launch traced here: 197 us
  blocking collectives  65.6 us (33%)
  other arithmetic  45.9 us (23%)
  waiting for transfers between devices  37.2 us (19%)
  local copies, waits for them, and re-layouts  25 us (13%)
  between operations  17 us (9%)
  starting transfers between devices  6.16 us (3%)
    psum x2, blocking collectives, local(): lax.psum((ahead_part, behind_part, length_part), 'atom')  65.6 us
    unnamed x2, waiting for transfers between devices  37.2 us
    scatter-add x1, other arithmetic, local(): partial_value = partial_value.at[:, pair_partner[0]].add(-pair_force)  21.1 us
    gather x1, local copies, waits for them, and re-layouts, local(): own_species = jnp.take(species, owner_local, axis=0)  19.5 us
    scatter-add x1, other arithmetic, local(): partial_value = partial_value.at[:, owner_atom].add(pair_force)  19.2 us
    ppermute x2, starting transfers between devices, passed_along(): return lax.ppermute(block, axis, route)  6.12 us
    unnamed x27, local copies, waits for them, and re-layouts  4.53 us
  transfers between devices with their start and end apart: 3, of which 1 were waited for; matrix products, arithmetic and copies ran while one was open for 33% of the time, Pallas kernels for 0%

commit v1 on v0

v1 whole, which is shorter than its diff:
```python
import functools

import jax
import jax.numpy as jnp
from jax import lax
from jax.experimental import pallas as pl
from jax.experimental.pallas import tpu as pltpu
from jax.sharding import PartitionSpec as P

MESH = pl.DeviceIdType.MESH
spring_const = 1.0
tangent_eps = 1e-06
WIDE = 256
LINES = 4


def step_kernel(
    n_img,
    n_atom,
    chunk,
    density,
    energy,
    dham,
    dovl,
    owner,
    partner,
    partner_species,
    count,
    species,
    orbitals,
    coords,
    reactant,
    product,
    band_out,
    tangent_out,
    dens_v,
    ener_v,
    dham_v,
    dovl_v,
    dens_f,
    ener_f,
    owner_v,
    partner_v,
    kind_v,
    count_s,
    species_v,
    orbitals_s,
    coords_v,
    ends_v,
    current_t,
    before_t,
    after_t,
    tan_all,
    part_all,
    recv_all,
    block_sem,
    small_sem,
    img_send,
    img_recv,
    tan_send,
    tan_recv,
    force_send,
    force_recv,
):
    f32, bf16, i32 = jnp.float32, jnp.bfloat16, jnp.int32
    img, me = lax.axis_index("img"), lax.axis_index("atom")
    n_slots = owner.shape[1]
    n_orb = density.shape[1]
    n_comp = dham.shape[3]
    n_kinds = orbitals.shape[0]
    rows_own = species.shape[0] // WIDE
    tile = rows_own * LINES
    n_chunks = n_slots // chunk

    smalls = [
        (owner, owner_v),
        (partner, partner_v),
        (partner_species, kind_v),
        (count, count_s),
        (species, species_v),
        (orbitals, orbitals_s),
        (coords, coords_v),
    ]
    small_copies = [
        pltpu.make_async_copy(src, dst, small_sem.at[i]) for i, (src, dst) in enumerate(smalls)
    ]
    for copy in small_copies:
        copy.start()
    ends = (
        pltpu.make_async_copy(reactant, ends_v.at[0], small_sem.at[len(smalls)]),
        pltpu.make_async_copy(product, ends_v.at[1], small_sem.at[len(smalls) + 1]),
    )
    first, last = img == 0, img == n_img - 1
    pl.when(first)(ends[0].start)
    pl.when(last)(ends[1].start)
    block_copies = []
    for k in range(n_chunks):
        cols = pl.ds(k * chunk, chunk)
        pairs = (
            (density.at[0, :, :, cols], dens_v.at[:, :, cols]),
            (energy.at[0, :, :, cols], ener_v.at[:, :, cols]),
            (dham.at[0, :, :, :, cols], dham_v.at[:, :, :, cols]),
            (dovl.at[0, :, :, :, cols], dovl_v.at[:, :, :, cols]),
        )
        block_copies.append(
            [pltpu.make_async_copy(s, d, block_sem.at[k, j]) for j, (s, d) in enumerate(pairs)]
        )
    for group in block_copies:
        for copy in group:
            copy.start()

    barrier = pltpu.get_barrier_semaphore()
    for s in range(1, n_atom):
        pl.semaphore_signal(
            barrier, inc=1, device_id={"atom": lax.rem(me + s, n_atom)}, device_id_type=MESH
        )

    @pl.when(img > 0)
    def _():
        pl.semaphore_signal(barrier, inc=1, device_id={"img": img - 1}, device_id_type=MESH)

    @pl.when(img < n_img - 1)
    def _():
        pl.semaphore_signal(barrier, inc=1, device_id={"img": img + 1}, device_id_type=MESH)

    for copy in small_copies:
        copy.wait()

    kinds_own = species_v[...].reshape(1, species.shape[0])
    table = jnp.zeros(kinds_own.shape, f32)
    for k in range(n_kinds):
        table = jnp.where(kinds_own == k, orbitals_s[k].astype(f32), table)
    table = jnp.concatenate(
        [table[:, h * WIDE : (h + 1) * WIDE] for h in range(rows_own)]
        + [jnp.zeros((16 - rows_own, WIDE), f32)],
        axis=0,
    ).astype(bf16)
    n_rows = n_atom * tile
    total = jnp.zeros((2 * n_rows, WIDE), f32)
    total_own = jnp.zeros((2 * tile, WIDE), f32)
    shift = WIDE.bit_length() - 1

    def onehot(low):
        return jnp.where(lax.broadcasted_iota(i32, (WIDE, chunk), 0) == low, 1.0, 0.0).astype(bf16)

    def work(k, total, total_own):
        cols = pl.ds(k * chunk, chunk)
        own = owner_v[:, cols]
        part = partner_v[:, cols]
        kind = kind_v[:, cols]
        own_hot = onehot(own & (WIDE - 1))
        part_hot = onehot(part & (WIDE - 1))
        own_row = own >> shift
        part_row = part >> shift
        picked = jnp.dot(table, own_hot, preferred_element_type=f32)
        own_orb = jnp.zeros((1, chunk), f32)
        for h in range(rows_own):
            own_orb = jnp.where(own_row == h, picked[h : h + 1], own_orb)
        part_orb = jnp.zeros((1, chunk), f32)
        for j in range(n_kinds):
            part_orb = jnp.where(kind == j, orbitals_s[j].astype(f32), part_orb)
        slot = lax.broadcasted_iota(i32, (1, chunk), 1) + k * chunk
        own_orb = jnp.where(slot < count_s[0, 0], own_orb, 0.0)
        level = lax.broadcasted_iota(i32, (n_orb, chunk), 0).astype(f32)
        for copy in block_copies[k]:
            copy.wait()
        for a in range(n_orb):
            bound = jnp.where(own_orb > a, part_orb, 0.0)
            mask = level < bound
            row = pl.ds(a * 16, n_orb)
            dens_f[row, :] = jnp.where(mask, dens_v[a, :, cols].astype(f32), 0.0)
            ener_f[row, :] = jnp.where(mask, ener_v[a, :, cols].astype(f32), 0.0)
        acc = [jnp.zeros((n_comp, chunk), f32) for _ in range(2)]
        for a in range(n_orb):
            for b in range(n_orb):
                row = pl.ds(a * 16 + b, 1)
                acc[0] = acc[0] + dens_f[row, :] * dham_v[a, b, :, cols].astype(f32)
                acc[1] = acc[1] + ener_f[row, :] * dovl_v[a, b, :, cols].astype(f32)
        force = -2.0 * (acc[0] - acc[1])
        line = lax.broadcasted_iota(i32, (tile, chunk), 0)
        lines = jnp.zeros((tile, chunk), f32)
        for c in range(n_comp):
            lines = jnp.where(line % LINES == c, force[c : c + 1], lines)
        upper = lines.astype(bf16).astype(f32)
        lower = lines - upper
        on_own = line // LINES == own_row
        lhs_own = jnp.concatenate(
            [jnp.where(on_own, upper, 0.0), jnp.where(on_own, lower, 0.0)], axis=0
        ).astype(bf16)
        pieces = []
        for value in (upper, lower):
            for d in range(n_atom):
                pieces.append(jnp.where(line // LINES + d * rows_own == part_row, value, 0.0))
        lhs = jnp.concatenate(pieces, axis=0).astype(bf16)
        dims = (((1,), (1,)), ((), ()))
        total = total + lax.dot_general(lhs, part_hot, dims, preferred_element_type=f32)
        total_own = total_own + lax.dot_general(lhs_own, own_hot, dims, preferred_element_type=f32)
        return total, total_own

    def to_next():
        return pltpu.make_async_remote_copy(
            src_ref=current_t,
            dst_ref=before_t,
            send_sem=img_send.at[0],
            recv_sem=img_recv.at[0],
            device_id={"img": img + 1},
            device_id_type=MESH,
        )

    def to_previous():
        return pltpu.make_async_remote_copy(
            src_ref=current_t,
            dst_ref=after_t,
            send_sem=img_send.at[1],
            recv_sem=img_recv.at[1],
            device_id={"img": img - 1},
            device_id_type=MESH,
        )

    def to_tile(ref, get):
        ref[...] = jnp.zeros_like(ref)
        for h in range(rows_own):
            for c in range(n_comp):
                row = h * LINES + c
                ref[row : row + 1, :] = get(c)[:, h * WIDE : (h + 1) * WIDE]

    def target(s):
        return lax.rem(me + s, n_atom)

    def tangent_copy(s):
        return pltpu.make_async_remote_copy(
            src_ref=tan_all.at[me],
            dst_ref=tan_all.at[me],
            send_sem=tan_send.at[s],
            recv_sem=tan_recv.at[me],
            device_id={"atom": target(s)},
            device_id_type=MESH,
        )

    def tangent_arrival(s):
        other = target(s)
        return pltpu.make_async_remote_copy(
            src_ref=tan_all.at[other],
            dst_ref=tan_all.at[other],
            send_sem=tan_send.at[s],
            recv_sem=tan_recv.at[other],
            device_id={"atom": other},
            device_id_type=MESH,
        )

    def force_copy(s):
        other = target(s)
        return pltpu.make_async_remote_copy(
            src_ref=part_all.at[other],
            dst_ref=recv_all.at[me],
            send_sem=force_send.at[s],
            recv_sem=force_recv.at[me],
            device_id={"atom": other},
            device_id_type=MESH,
        )

    def force_arrival(s):
        other = target(s)
        return pltpu.make_async_remote_copy(
            src_ref=part_all.at[other],
            dst_ref=recv_all.at[other],
            send_sem=force_send.at[s],
            recv_sem=force_recv.at[other],
            device_id={"atom": other},
            device_id_type=MESH,
        )

    tile_line = lax.broadcasted_iota(i32, (tile, WIDE), 0)
    greeted = (n_atom - 1) + jnp.where(img > 0, 1, 0) + jnp.where(img < n_img - 1, 1, 0)

    def send_coords():
        to_tile(current_t, lambda c: coords_v[c])
        pl.semaphore_wait(barrier, greeted)
        pl.when(img < n_img - 1)(lambda: to_next().start())
        pl.when(img > 0)(lambda: to_previous().start())

    def send_tangent():
        @pl.when(first)
        def _():
            ends[0].wait()
            to_tile(before_t, lambda c: ends_v[0, c : c + 1])

        @pl.when(last)
        def _():
            ends[1].wait()
            to_tile(after_t, lambda c: ends_v[1, c : c + 1])

        pl.when(img > 0)(lambda: to_next().wait_recv())
        pl.when(img < n_img - 1)(lambda: to_previous().wait_recv())
        current, before, after = current_t[...], before_t[...], after_t[...]
        ahead = jnp.sum((after - current) ** 2, axis=0, keepdims=True)
        behind = jnp.sum((current - before) ** 2, axis=0, keepdims=True)
        mine = after - before
        mine = jnp.where(tile_line == LINES - 1, ahead, mine)
        mine = jnp.where(tile_line == 2 * LINES - 1, behind, mine)
        tan_all[me] = mine
        for s in range(1, n_atom):
            tangent_copy(s).start()

    early = min(1, n_chunks - 1)
    middle = min(3, n_chunks - 1)
    for k in range(n_chunks):
        if k == early:
            send_coords()
        if k == middle:
            send_tangent()
        total, total_own = work(k, total, total_own)

    for s in range(1, n_atom):
        tangent_arrival(s).wait_recv()
    partner_sum = total[:n_rows] + total[n_rows:]
    own_sum = total_own[:tile] + total_own[tile:]
    plain = tile_line % LINES < n_comp
    parts, dot = [], jnp.zeros((tile, WIDE), f32)
    square = jnp.zeros((tile, WIDE), f32)
    sums = jnp.zeros((tile, WIDE), f32)
    for d in range(n_atom):
        value = jnp.where(me == d, own_sum, 0.0) - partner_sum[d * tile : (d + 1) * tile]
        other = tan_all[d]
        tangent = jnp.where(plain, other, 0.0)
        dot = dot + value * tangent
        square = square + tangent * tangent
        sums = sums + other
        parts.append(value)
    dot = jnp.sum(dot, axis=0, keepdims=True)
    for d in range(n_atom):
        part_all[d] = jnp.where(tile_line == LINES - 1, dot, parts[d])
    for s in range(1, n_atom):
        force_copy(s).start()
    recv_all[me] = part_all[me]
    length = jnp.sum(square, keepdims=True)
    ahead = jnp.sum(sums[LINES - 1 : LINES], keepdims=True)
    behind = jnp.sum(sums[2 * LINES - 1 : 2 * LINES], keepdims=True)
    inverse = 1.0 / jnp.sqrt(length + tangent_eps)
    spring = spring_const * (jnp.sqrt(ahead) - jnp.sqrt(behind))
    for s in range(1, n_atom):
        force_arrival(s).wait_recv()
    summed = recv_all[0]
    for d in range(1, n_atom):
        summed = summed + recv_all[d]
    along = jnp.sum(summed[LINES - 1 : LINES], keepdims=True) * inverse
    band = summed + ((spring - along) * inverse) * tan_all[me]
    for h in range(rows_own):
        for c in range(n_comp):
            row = h * LINES + c
            band_out[c, :, h * WIDE : (h + 1) * WIDE] = band[row : row + 1]
    tangent_out[...] = along
    pl.when(img < n_img - 1)(lambda: to_next().wait_send())
    pl.when(img > 0)(lambda: to_previous().wait_send())
    for s in range(1, n_atom):
        tangent_copy(s).wait_send()
        force_copy(s).wait_send()


def solution(mesh):
    n_img, n_atom = mesh.shape["img"], mesh.shape["atom"]

    def local(density, energy, dham, dovl, owner, partner, kind, count, species, *rest):
        orbitals, coords, reactant, product = rest
        dham, dovl = (jnp.transpose(x, (0, 2, 3, 1, 4)) for x in (dham, dovl))
        coords = jnp.transpose(coords, (1, 0, 2))
        args = (density, energy, dham, dovl, owner, partner, kind, count, species)
        args += (orbitals, coords, reactant, product)
        n_slots, n_orb = owner.shape[1], density.shape[1]
        chunk = next(c for c in (512, 256, 128) if n_slots % c == 0)
        tile = species.shape[0] // WIDE * LINES
        tiles = (n_atom, tile, WIDE)
        dma = pltpu.SemaphoreType.DMA
        band, along = pl.pallas_call(
            functools.partial(step_kernel, n_img, n_atom, chunk),
            out_shape=(
                jax.ShapeDtypeStruct(coords.shape, jnp.float32),
                jax.ShapeDtypeStruct((1, 1), jnp.float32),
            ),
            in_specs=[pl.BlockSpec(memory_space=pltpu.HBM)] * len(args),
            out_specs=(
                pl.BlockSpec(memory_space=pltpu.VMEM),
                pl.BlockSpec(memory_space=pltpu.VMEM),
            ),
            scratch_shapes=[
                pltpu.VMEM(density.shape[1:], jnp.bfloat16),
                pltpu.VMEM(density.shape[1:], jnp.bfloat16),
                pltpu.VMEM(dham.shape[1:], jnp.bfloat16),
                pltpu.VMEM(dham.shape[1:], jnp.bfloat16),
                pltpu.VMEM((n_orb * 16, chunk), jnp.float32),
                pltpu.VMEM((n_orb * 16, chunk), jnp.float32),
                pltpu.VMEM(owner.shape, jnp.int32),
                pltpu.VMEM(owner.shape, jnp.int32),
                pltpu.VMEM(owner.shape, jnp.int32),
                pltpu.SMEM(count.shape, jnp.int32),
                pltpu.VMEM(species.shape, jnp.int32),
                pltpu.SMEM(orbitals.shape, jnp.int32),
                pltpu.VMEM(coords.shape, jnp.float32),
                pltpu.VMEM((2,) + reactant.shape, jnp.float32),
                pltpu.VMEM(tiles[1:], jnp.float32),
                pltpu.VMEM(tiles[1:], jnp.float32),
                pltpu.VMEM(tiles[1:], jnp.float32),
                pltpu.VMEM(tiles, jnp.float32),
                pltpu.VMEM(tiles, jnp.float32),
                pltpu.VMEM(tiles, jnp.float32),
                dma((n_slots // chunk, 4)),
                dma((9,)),
                dma((2,)),
                dma((2,)),
                dma((n_atom,)),
                dma((n_atom,)),
                dma((n_atom,)),
                dma((n_atom,)),
            ],
            compiler_params=pltpu.CompilerParams(
                collective_id=0, has_side_effects=True, vmem_limit_bytes=63 * 1024 * 1024
            ),
        )(*args)
        return jnp.transpose(band, (1, 0, 2)), jnp.reshape(along, (1,))

    return jax.shard_map(
        local,
        mesh=mesh,
        in_specs=(
            P("img", None, None, "atom"),
            P("img", None, None, "atom"),
            P("img", None, None, None, "atom"),
            P("img", None, None, None, "atom"),
            P("img", "atom"),
            P("img", "atom"),
            P("img", "atom"),
            P("img", "atom"),
            P("atom"),
            P(),
            P("img", None, "atom"),
            P(None, "atom"),
            P(None, "atom"),
        ),
        out_specs=(P("img", None, "atom"), P("img")),
        check_vma=False,
    )
```

time: 198 us -> 24.5 us (0.12)
  blocking collectives: 65.6 us -> 0 us
  other arithmetic: 45.9 us -> 0 us
  waiting for transfers between devices: 37.2 us -> 0 us
  local copies, waits for them, and re-layouts: 25 us -> 1.29 us
  Pallas kernels: 0 us -> 20 us
  between operations: 17 us -> 3.05 us
  starting transfers between devices: 6.16 us -> 0 us
    psum x2 -> x0, blocking collectives: 65.6 us -> none  [local(): lax.psum((ahead_part, behind_part, length_part), 'atom')]
    scatter-add x2 -> x0, other arithmetic: 40.2 us -> none  [the longest x1 21.1 us: local(): partial_value = partial_value.at[:, pair_partner[0]].add(-pair_force)]
    unnamed x2 -> x0, waiting for transfers between devices: 37.2 us -> none
    pallas_call x0 -> x1, Pallas kernels: none -> 20 us  [local(): pl.pallas_call(functools.partial(step_kernel, n_img, n_atom, chunk), out_...]
    gather x1 -> x0, local copies, waits for them, and re-layouts: 19.5 us -> none  [local(): own_species = jnp.take(species, owner_local, axis=0)]
    ppermute x2 -> x0, starting transfers between devices: 6.12 us -> none  [passed_along(): return lax.ppermute(block, axis, route)]
    unnamed x27 -> x1, local copies, waits for them, and re-layouts: 4.53 us -> 1.29 us
    unnamed x3 -> x0, other arithmetic: 2.82 us -> none
  transfers between devices with their start and end apart: 3 -> 0, of which waited for: 1 -> 0; matrix products, arithmetic and copies ran while one was open for 33% -> 0% of each run, Pallas kernels for 0% -> 0%
where the time goes in v1:
time: 24.5 us; the launch traced here: 24.3 us
  Pallas kernels  20 us (82%)
  between operations  3.05 us (12%)
  local copies, waits for them, and re-layouts  1.29 us (5%)
    pallas_call x1, Pallas kernels, local(): pl.pallas_call(functools.partial(step_kernel, n_img, n_atom, chunk), out_...  20 us
    unnamed x1, local copies, waits for them, and re-layouts  1.29 us

profile of v1, /device:TPU:0, one launch (start us, length us, event | category | flops | bytes accessed | tf_op | source)
XLA Modules:
  0.0 24.3 jit_solution(11031601522267307047)
XLA Ops:
  1.3 20.0 %shard_map.140 = (f32[3,1,512]{2,1,0:T(1,128)}, f32[1,1]{1,0:T(1,128)}) custom-call(bf16[1,9,9,3072]{3,2,1,0:T(8,128)(2,1)} %density.1, bf16[1,9,9,3072]{3,2,1,0:T(8,128)(2,1)} %energy.1, bf16[1,9,9,3,3072]{4,3,2,1,0:T(4,128)(2,1)} %bitcast.5, bf16[1,9,9,3,3072]{4,3,2,1,0:T(4,128)(2,1)} %bitcast.6, s32[1,3072]{1,0:T(1,128)} %owner.1, s32[1,3072]{1,0:T(1,128)} %partner.1, ...), custom_call_target="tpu_custom_call" | custom-call | tf_op jit(solution)/shard_map/pallas_call | solution.py:374
  21.3 1.3 %copy.18 = f32[1,3,512]{2,0,1:T(1,128)} copy(f32[1,3,512]{2,0,1:T(1,128)} %bitcast.7) | data formatting | bytes 12288

commit v2 on v1

--- a/solution.py
+++ b/solution.py
@@ -31,7 +31,8 @@
     coords,
     reactant,
     product,
-    band_out,
+    force_out,
+    pull_out,
     tangent_out,
     dens_v,
     ener_v,
@@ -39,6 +40,11 @@
     dovl_v,
     dens_f,
     ener_f,
+    own_hot,
+    part_hot,
+    orb_v,
+    total,
+    total_own,
     owner_v,
     partner_v,
     kind_v,
@@ -93,21 +99,22 @@
     first, last = img == 0, img == n_img - 1
     pl.when(first)(ends[0].start)
     pl.when(last)(ends[1].start)
-    block_copies = []
-    for k in range(n_chunks):
-        cols = pl.ds(k * chunk, chunk)
-        pairs = (
+
+    def block_pairs(k):
+        cols = pl.ds(k * chunk if isinstance(k, int) else pl.multiple_of(k * chunk, chunk), chunk)
+        return (
             (density.at[0, :, :, cols], dens_v.at[:, :, cols]),
             (energy.at[0, :, :, cols], ener_v.at[:, :, cols]),
             (dham.at[0, :, :, :, cols], dham_v.at[:, :, :, cols]),
             (dovl.at[0, :, :, :, cols], dovl_v.at[:, :, :, cols]),
         )
-        block_copies.append(
-            [pltpu.make_async_copy(s, d, block_sem.at[k, j]) for j, (s, d) in enumerate(pairs)]
-        )
-    for group in block_copies:
-        for copy in group:
-            copy.start()
+
+    def fetch(k, carry):
+        for j, (src, dst) in enumerate(block_pairs(k)):
+            pltpu.make_async_copy(src, dst, block_sem.at[k, j]).start()
+        return carry
+
+    lax.fori_loop(0, n_chunks, fetch, 0)
 
     barrier = pltpu.get_barrier_semaphore()
     for s in range(1, n_atom):
@@ -136,23 +143,34 @@
         axis=0,
     ).astype(bf16)
     n_rows = n_atom * tile
-    total = jnp.zeros((2 * n_rows, WIDE), f32)
-    total_own = jnp.zeros((2 * tile, WIDE), f32)
     shift = WIDE.bit_length() - 1
-
-    def onehot(low):
-        return jnp.where(lax.broadcasted_iota(i32, (WIDE, chunk), 0) == low, 1.0, 0.0).astype(bf16)
-
-    def work(k, total, total_own):
-        cols = pl.ds(k * chunk, chunk)
+    pack = 16
+    dims = (((1,), (1,)), ((), ()))
+    zero = jnp.zeros((), bf16)
+    pack_line = lax.broadcasted_iota(i32, (pack, chunk), 0)
+    pack_row = pack_line.astype(f32).astype(bf16)
+    atom_row = (pack_line // LINES).astype(f32).astype(bf16)
+    own_atom_row = (pack_line % tile // LINES).astype(f32).astype(bf16)
+    level = lax.broadcasted_iota(i32, (n_orb, chunk), 0).astype(f32).astype(bf16)
+
+    def columns(k):
+        return pl.ds(pl.multiple_of(k * chunk, chunk), chunk)
+
+    def small(values):
+        return values.astype(f32).astype(bf16)
+
+    def prepare(k, carry):
+        cols = columns(k)
         own = owner_v[:, cols]
         part = partner_v[:, cols]
         kind = kind_v[:, cols]
-        own_hot = onehot(own & (WIDE - 1))
-        part_hot = onehot(part & (WIDE - 1))
+        for index, hot in ((own, own_hot), (part, part_hot)):
+            low = jnp.broadcast_to(small(index & (WIDE - 1)), (pack, chunk))
+            for g in range(WIDE // pack):
+                match = pack_row == low - jnp.asarray(g * pack, bf16)
+                hot[g * pack : (g + 1) * pack, cols] = jnp.where(match, zero + 1, zero)
         own_row = own >> shift
-        part_row = part >> shift
-        picked = jnp.dot(table, own_hot, preferred_element_type=f32)
+        picked = jnp.dot(table, own_hot[:, cols], preferred_element_type=f32)
         own_orb = jnp.zeros((1, chunk), f32)
         for h in range(rows_own):
             own_orb = jnp.where(own_row == h, picked[h : h + 1], own_orb)
@@ -160,16 +178,22 @@
         for j in range(n_kinds):
             part_orb = jnp.where(kind == j, orbitals_s[j].astype(f32), part_orb)
         slot = lax.broadcasted_iota(i32, (1, chunk), 1) + k * chunk
-        own_orb = jnp.where(slot < count_s[0, 0], own_orb, 0.0)
-        level = lax.broadcasted_iota(i32, (n_orb, chunk), 0).astype(f32)
-        for copy in block_copies[k]:
-            copy.wait()
+        orb_v[0:1, cols] = jnp.where(slot < count_s[0, 0], own_orb, 0.0)
+        orb_v[1:2, cols] = part_orb
+        return carry
+
+    def work(k, carry):
+        pl.when(k == middle)(send_tangent)
+        cols = columns(k)
+        own_orb, part_orb = orb_v[0:1, cols], orb_v[1:2, cols]
+        for j, (src, dst) in enumerate(block_pairs(k)):
+            pltpu.make_async_copy(src, dst, block_sem.at[k, j]).wait()
         for a in range(n_orb):
-            bound = jnp.where(own_orb > a, part_orb, 0.0)
+            bound = jnp.where(own_orb > a, part_orb, 0.0).astype(bf16)
             mask = level < bound
             row = pl.ds(a * 16, n_orb)
-            dens_f[row, :] = jnp.where(mask, dens_v[a, :, cols].astype(f32), 0.0)
-            ener_f[row, :] = jnp.where(mask, ener_v[a, :, cols].astype(f32), 0.0)
+            dens_f[row, :] = jnp.where(mask, dens_v[a, :, cols], zero).astype(f32)
+            ener_f[row, :] = jnp.where(mask, ener_v[a, :, cols], zero).astype(f32)
         acc = [jnp.zeros((n_comp, chunk), f32) for _ in range(2)]
         for a in range(n_orb):
             for b in range(n_orb):
@@ -183,19 +207,22 @@
             lines = jnp.where(line % LINES == c, force[c : c + 1], lines)
         upper = lines.astype(bf16).astype(f32)
         lower = lines - upper
-        on_own = line // LINES == own_row
-        lhs_own = jnp.concatenate(
-            [jnp.where(on_own, upper, 0.0), jnp.where(on_own, lower, 0.0)], axis=0
-        ).astype(bf16)
-        pieces = []
-        for value in (upper, lower):
-            for d in range(n_atom):
-                pieces.append(jnp.where(line // LINES + d * rows_own == part_row, value, 0.0))
-        lhs = jnp.concatenate(pieces, axis=0).astype(bf16)
-        dims = (((1,), (1,)), ((), ()))
-        total = total + lax.dot_general(lhs, part_hot, dims, preferred_element_type=f32)
-        total_own = total_own + lax.dot_general(lhs_own, own_hot, dims, preferred_element_type=f32)
-        return total, total_own
+        own_row = jnp.broadcast_to(small(owner_v[:, cols] >> shift), (pack, chunk))
+        part_row = jnp.broadcast_to(small(partner_v[:, cols] >> shift), (pack, chunk))
+        both = jnp.concatenate([upper, lower], axis=0).astype(bf16)
+        lhs_own = jnp.where(own_atom_row == own_row, both, zero)
+        twice = [jnp.concatenate([v] * (pack // tile), axis=0).astype(bf16) for v in (upper, lower)]
+        uppers, lowers = [], []
+        for g in range(n_rows // pack):
+            match = atom_row == part_row - jnp.asarray(g * (pack // LINES), bf16)
+            uppers.append(jnp.where(match, twice[0], zero))
+            lowers.append(jnp.where(match, twice[1], zero))
+        lhs = jnp.concatenate(uppers + lowers, axis=0)
+        total[...] += lax.dot_general(lhs, part_hot[:, cols], dims, preferred_element_type=f32)
+        total_own[...] += lax.dot_general(
+            lhs_own, own_hot[:, cols], dims, preferred_element_type=f32
+        )
+        return carry
 
     def to_next():
         return pltpu.make_async_remote_copy(
@@ -302,19 +329,17 @@
         for s in range(1, n_atom):
             tangent_copy(s).start()
 
-    early = min(1, n_chunks - 1)
-    middle = min(3, n_chunks - 1)
-    for k in range(n_chunks):
-        if k == early:
-            send_coords()
-        if k == middle:
-            send_tangent()
-        total, total_own = work(k, total, total_own)
+    middle = min(2, n_chunks - 1)
+    total[...] = jnp.zeros_like(total)
+    total_own[...] = jnp.zeros_like(total_own)
+    lax.fori_loop(0, n_chunks, prepare, 0)
+    send_coords()
+    lax.fori_loop(0, n_chunks, work, 0)
 
     for s in range(1, n_atom):
         tangent_arrival(s).wait_recv()
-    partner_sum = total[:n_rows] + total[n_rows:]
-    own_sum = total_own[:tile] + total_own[tile:]
+    partner_sum = total[:n_rows, :] + total[n_rows:, :]
+    own_sum = total_own[:tile, :] + total_own[tile:, :]
     plain = tile_line % LINES < n_comp
     parts, dot = [], jnp.zeros((tile, WIDE), f32)
     square = jnp.zeros((tile, WIDE), f32)
@@ -344,11 +369,12 @@
     for d in range(1, n_atom):
         summed = summed + recv_all[d]
     along = jnp.sum(summed[LINES - 1 : LINES], keepdims=True) * inverse
-    band = summed + ((spring - along) * inverse) * tan_all[me]
+    pull = ((spring - along) * inverse) * tan_all[me]
     for h in range(rows_own):
         for c in range(n_comp):
             row = h * LINES + c
-            band_out[c, :, h * WIDE : (h + 1) * WIDE] = band[row : row + 1]
+            force_out[c, :, h * WIDE : (h + 1) * WIDE] = summed[row : row + 1]
+            pull_out[c, :, h * WIDE : (h + 1) * WIDE] = pull[row : row + 1]
     tangent_out[...] = along
     pl.when(img < n_img - 1)(lambda: to_next().wait_send())
     pl.when(img > 0)(lambda: to_previous().wait_send())
@@ -371,14 +397,16 @@
         tile = species.shape[0] // WIDE * LINES
         tiles = (n_atom, tile, WIDE)
         dma = pltpu.SemaphoreType.DMA
-        band, along = pl.pallas_call(
+        force, pull, along = pl.pallas_call(
             functools.partial(step_kernel, n_img, n_atom, chunk),
             out_shape=(
+                jax.ShapeDtypeStruct(coords.shape, jnp.float32),
                 jax.ShapeDtypeStruct(coords.shape, jnp.float32),
                 jax.ShapeDtypeStruct((1, 1), jnp.float32),
             ),
             in_specs=[pl.BlockSpec(memory_space=pltpu.HBM)] * len(args),
             out_specs=(
+                pl.BlockSpec(memory_space=pltpu.VMEM),
                 pl.BlockSpec(memory_space=pltpu.VMEM),
                 pl.BlockSpec(memory_space=pltpu.VMEM),
             ),
@@ -389,6 +417,11 @@
                 pltpu.VMEM(dham.shape[1:], jnp.bfloat16),
                 pltpu.VMEM((n_orb * 16, chunk), jnp.float32),
                 pltpu.VMEM((n_orb * 16, chunk), jnp.float32),
+                pltpu.VMEM((WIDE, n_slots), jnp.bfloat16),
+                pltpu.VMEM((WIDE, n_slots), jnp.bfloat16),
+                pltpu.VMEM((8, n_slots), jnp.float32),
+                pltpu.VMEM((2 * n_atom * tile, WIDE), jnp.float32),
+                pltpu.VMEM((2 * tile, WIDE), jnp.float32),
                 pltpu.VMEM(owner.shape, jnp.int32),
                 pltpu.VMEM(owner.shape, jnp.int32),
                 pltpu.VMEM(owner.shape, jnp.int32),
@@ -416,7 +449,7 @@
                 collective_id=0, has_side_effects=True, vmem_limit_bytes=63 * 1024 * 1024
             ),
         )(*args)
-        return jnp.transpose(band, (1, 0, 2)), jnp.reshape(along, (1,))
+        return jnp.transpose(force + pull, (1, 0, 2)), jnp.reshape(along, (1,))
 
     return jax.shard_map(
         local,

time: 24.5 us -> 24.8 us (1.012)
  other arithmetic: 0 us -> 1.31 us
  local copies, waits for them, and re-layouts: 1.29 us -> 0 us
    transpose x0 -> x1, other arithmetic: none -> 1.31 us  [local(): return (jnp.transpose(force + pull, (1, 0, 2)), jnp.reshape(along, (1,)))]
    unnamed x1 -> x0, local copies, waits for them, and re-layouts: 1.29 us -> none
where the time goes in v2:
time: 24.8 us; the launch traced here: 24.4 us
  Pallas kernels  20.1 us (81%)
  between operations  3.05 us (12%)
  other arithmetic  1.31 us (5%)
    pallas_call x1, Pallas kernels, local(): pl.pallas_call(functools.partial(step_kernel, n_img, n_atom, chunk), out_...  20.1 us
    transpose x1, other arithmetic, local(): return (jnp.transpose(force + pull, (1, 0, 2)), jnp.reshape(along, (1,)))  1.31 us

profile of v2, /device:TPU:0, one launch (start us, length us, event | category | flops | bytes accessed | tf_op | source)
XLA Modules:
  0.0 24.4 jit_solution(838994182363760630)
XLA Ops:
  1.3 20.1 %shard_map.140 = (f32[3,1,512]{2,1,0:T(1,128)}, f32[3,1,512]{2,1,0:T(1,128)}, f32[1,1]{1,0:T(1,128)}) custom-call(bf16[1,9,9,3072]{3,2,1,0:T(8,128)(2,1)} %density.1, bf16[1,9,9,3072]{3,2,1,0:T(8,128)(2,1)} %energy.1, bf16[1,9,9,3,3072]{4,3,2,1,0:T(4,128)(2,1)} %bitcast.6, bf16[1,9,9,3,3072]{4,3,2,1,0:T(4,128)(2,1)} %bitcast.7, s32[1,3072]{1,0:T(1,128)} %owner.1, ...), custom_call_target="tpu_custom_call" | custom-call | tf_op jit(solution)/shard_map/pallas_call | solution.py:400
  21.3 1.3 %add_bitcast_fusion = f32[1,3,512]{2,0,1:T(1,128)} fusion(f32[3,1,512]{2,1,0:T(1,128)} %get-tuple-element.5, f32[3,1,512]{2,1,0:T(1,128)} %get-tuple-element.6), kind=kLoop, calls=%fused_computation | loop fusion | flops 1536 | bytes 18432 | tf_op jit(solution)/shard_map/transpose | solution.py:452

commit v3 on v2

--- a/solution.py
+++ b/solution.py
@@ -31,8 +31,7 @@
     coords,
     reactant,
     product,
-    force_out,
-    pull_out,
+    band_out,
     tangent_out,
     dens_v,
     ener_v,
@@ -58,7 +57,9 @@
     after_t,
     tan_all,
     part_all,
-    recv_all,
+    near_sums,
+    middle_sums,
+    far_sums,
     block_sem,
     small_sem,
     img_send,
@@ -70,6 +71,9 @@
 ):
     f32, bf16, i32 = jnp.float32, jnp.bfloat16, jnp.int32
     img, me = lax.axis_index("img"), lax.axis_index("atom")
+    n_lo = max(f for f in range(1, n_atom + 1) if n_atom % f == 0 and f * f <= n_atom)
+    n_hi = n_atom // n_lo
+    hi, lo = me // n_lo, lax.rem(me, n_lo)
     n_slots = owner.shape[1]
     n_orb = density.shape[1]
     n_comp = dham.shape[3]
@@ -77,6 +81,14 @@
     rows_own = species.shape[0] // WIDE
     tile = rows_own * LINES
     n_chunks = n_slots // chunk
+
+    def near(s):
+        other = lax.rem(lo + s, n_lo)
+        return other, hi * n_lo + other
+
+    def far(s):
+        other = lax.rem(hi + s, n_hi)
+        return other, other * n_lo + lo
 
     smalls = [
         (owner, owner_v),
@@ -117,10 +129,10 @@
     lax.fori_loop(0, n_chunks, fetch, 0)
 
     barrier = pltpu.get_barrier_semaphore()
-    for s in range(1, n_atom):
-        pl.semaphore_signal(
-            barrier, inc=1, device_id={"atom": lax.rem(me + s, n_atom)}, device_id_type=MESH
-        )
+    for s in range(1, n_lo):
+        pl.semaphore_signal(barrier, inc=1, device_id={"atom": near(s)[1]}, device_id_type=MESH)
+    for s in range(1, n_hi):
+        pl.semaphore_signal(barrier, inc=1, device_id={"atom": far(s)[1]}, device_id_type=MESH)
 
     @pl.when(img > 0)
     def _():
@@ -184,6 +196,7 @@
 
     def work(k, carry):
         pl.when(k == middle)(send_tangent)
+        pl.when(k == late)(pass_tangents)
         cols = columns(k)
         own_orb, part_orb = orb_v[0:1, cols], orb_v[1:2, cols]
         for j, (src, dst) in enumerate(block_pairs(k)):
@@ -251,54 +264,46 @@
                 row = h * LINES + c
                 ref[row : row + 1, :] = get(c)[:, h * WIDE : (h + 1) * WIDE]
 
-    def target(s):
-        return lax.rem(me + s, n_atom)
-
-    def tangent_copy(s):
+    def remote(src, dst, send, recv, device):
         return pltpu.make_async_remote_copy(
-            src_ref=tan_all.at[me],
-            dst_ref=tan_all.at[me],
-            send_sem=tan_send.at[s],
-            recv_sem=tan_recv.at[me],
-            device_id={"atom": target(s)},
+            src_ref=src,
+            dst_ref=dst,
+            send_sem=send,
+            recv_sem=recv,
+            device_id={"atom": device},
             device_id_type=MESH,
         )
 
-    def tangent_arrival(s):
-        other = target(s)
-        return pltpu.make_async_remote_copy(
-            src_ref=tan_all.at[other],
-            dst_ref=tan_all.at[other],
-            send_sem=tan_send.at[s],
-            recv_sem=tan_recv.at[other],
-            device_id={"atom": other},
-            device_id_type=MESH,
-        )
-
-    def force_copy(s):
-        other = target(s)
-        return pltpu.make_async_remote_copy(
-            src_ref=part_all.at[other],
-            dst_ref=recv_all.at[me],
-            send_sem=force_send.at[s],
-            recv_sem=force_recv.at[me],
-            device_id={"atom": other},
-            device_id_type=MESH,
-        )
-
-    def force_arrival(s):
-        other = target(s)
-        return pltpu.make_async_remote_copy(
-            src_ref=part_all.at[other],
-            dst_ref=recv_all.at[other],
-            send_sem=force_send.at[s],
-            recv_sem=force_recv.at[other],
-            device_id={"atom": other},
-            device_id_type=MESH,
+    def tan_near(s, slot):
+        place = tan_all.at[hi, slot]
+        return remote(place, place, tan_send.at[0, s], tan_recv.at[0, slot], near(s)[1])
+
+    def tan_far(s, slot):
+        place = tan_all.at[slot]
+        return remote(place, place, tan_send.at[1, s], tan_recv.at[1, slot], far(s)[1])
+
+    def force_near(s, slot):
+        other, device = near(s)
+        return remote(
+            part_all.at[:, other],
+            near_sums.at[slot],
+            force_send.at[0, s],
+            force_recv.at[0, slot],
+            device,
+        )
+
+    def force_far(s, slot):
+        other, device = far(s)
+        return remote(
+            middle_sums.at[other],
+            far_sums.at[slot],
+            force_send.at[1, s],
+            force_recv.at[1, slot],
+            device,
         )
 
     tile_line = lax.broadcasted_iota(i32, (tile, WIDE), 0)
-    greeted = (n_atom - 1) + jnp.where(img > 0, 1, 0) + jnp.where(img < n_img - 1, 1, 0)
+    greeted = (n_lo - 1) + (n_hi - 1) + jnp.where(img > 0, 1, 0) + jnp.where(img < n_img - 1, 1, 0)
 
     def send_coords():
         to_tile(current_t, lambda c: coords_v[c])
@@ -325,19 +330,25 @@
         mine = after - before
         mine = jnp.where(tile_line == LINES - 1, ahead, mine)
         mine = jnp.where(tile_line == 2 * LINES - 1, behind, mine)
-        tan_all[me] = mine
-        for s in range(1, n_atom):
-            tangent_copy(s).start()
-
-    middle = min(2, n_chunks - 1)
+        tan_all[hi, lo] = mine
+        for s in range(1, n_lo):
+            tan_near(s, lo).start()
+
+    def pass_tangents():
+        for s in range(1, n_lo):
+            tan_near(s, near(s)[0]).wait_recv()
+        for s in range(1, n_hi):
+            tan_far(s, hi).start()
+
+    middle, late = min(2, n_chunks - 1), min(4, n_chunks - 1)
     total[...] = jnp.zeros_like(total)
     total_own[...] = jnp.zeros_like(total_own)
     lax.fori_loop(0, n_chunks, prepare, 0)
     send_coords()
     lax.fori_loop(0, n_chunks, work, 0)
 
-    for s in range(1, n_atom):
-        tangent_arrival(s).wait_recv()
+    for s in range(1, n_hi):
+        tan_far(s, far(s)[0]).wait_recv()
     partner_sum = total[:n_rows, :] + total[n_rows:, :]
     own_sum = total_own[:tile, :] + total_own[tile:, :]
     plain = tile_line % LINES < n_comp
@@ -346,7 +357,7 @@
     sums = jnp.zeros((tile, WIDE), f32)
     for d in range(n_atom):
         value = jnp.where(me == d, own_sum, 0.0) - partner_sum[d * tile : (d + 1) * tile]
-        other = tan_all[d]
+        other = tan_all[d // n_lo, d % n_lo]
         tangent = jnp.where(plain, other, 0.0)
         dot = dot + value * tangent
         square = square + tangent * tangent
@@ -354,33 +365,42 @@
         parts.append(value)
     dot = jnp.sum(dot, axis=0, keepdims=True)
     for d in range(n_atom):
-        part_all[d] = jnp.where(tile_line == LINES - 1, dot, parts[d])
-    for s in range(1, n_atom):
-        force_copy(s).start()
-    recv_all[me] = part_all[me]
+        part_all[d // n_lo, d % n_lo] = jnp.where(tile_line == LINES - 1, dot, parts[d])
+    for s in range(1, n_lo):
+        force_near(s, lo).start()
     length = jnp.sum(square, keepdims=True)
     ahead = jnp.sum(sums[LINES - 1 : LINES], keepdims=True)
     behind = jnp.sum(sums[2 * LINES - 1 : 2 * LINES], keepdims=True)
     inverse = 1.0 / jnp.sqrt(length + tangent_eps)
     spring = spring_const * (jnp.sqrt(ahead) - jnp.sqrt(behind))
-    for s in range(1, n_atom):
-        force_arrival(s).wait_recv()
-    summed = recv_all[0]
-    for d in range(1, n_atom):
-        summed = summed + recv_all[d]
+    mine = part_all[:, lo]
+    for s in range(1, n_lo):
+        other = near(s)[0]
+        force_near(s, other).wait_recv()
+        mine = mine + near_sums[other]
+    middle_sums[...] = mine
+    for s in range(1, n_hi):
+        force_far(s, hi).start()
+    summed = middle_sums[hi]
+    for s in range(1, n_hi):
+        other = far(s)[0]
+        force_far(s, other).wait_recv()
+        summed = summed + far_sums[other]
     along = jnp.sum(summed[LINES - 1 : LINES], keepdims=True) * inverse
-    pull = ((spring - along) * inverse) * tan_all[me]
+    band = summed + ((spring - along) * inverse) * tan_all[hi, lo]
     for h in range(rows_own):
         for c in range(n_comp):
             row = h * LINES + c
-            force_out[c, :, h * WIDE : (h + 1) * WIDE] = summed[row : row + 1]
-            pull_out[c, :, h * WIDE : (h + 1) * WIDE] = pull[row : row + 1]
+            band_out[c, :, h * WIDE : (h + 1) * WIDE] = band[row : row + 1]
     tangent_out[...] = along
     pl.when(img < n_img - 1)(lambda: to_next().wait_send())
     pl.when(img > 0)(lambda: to_previous().wait_send())
-    for s in range(1, n_atom):
-        tangent_copy(s).wait_send()
-        force_copy(s).wait_send()
+    for s in range(1, n_lo):
+        tan_near(s, lo).wait_send()
+        force_near(s, lo).wait_send()
+    for s in range(1, n_hi):
+        tan_far(s, hi).wait_send()
+        force_far(s, hi).wait_send()
 
 
 def solution(mesh):
@@ -395,18 +415,18 @@
         n_slots, n_orb = owner.shape[1], density.shape[1]
         chunk = next(c for c in (512, 256, 128) if n_slots % c == 0)
         tile = species.shape[0] // WIDE * LINES
-        tiles = (n_atom, tile, WIDE)
+        n_lo = max(f for f in range(1, n_atom + 1) if n_atom % f == 0 and f * f <= n_atom)
+        n_hi = n_atom // n_lo
+        tiles = (tile, WIDE)
         dma = pltpu.SemaphoreType.DMA
-        force, pull, along = pl.pallas_call(
+        band, along = pl.pallas_call(
             functools.partial(step_kernel, n_img, n_atom, chunk),
             out_shape=(
-                jax.ShapeDtypeStruct(coords.shape, jnp.float32),
                 jax.ShapeDtypeStruct(coords.shape, jnp.float32),
                 jax.ShapeDtypeStruct((1, 1), jnp.float32),
             ),
             in_specs=[pl.BlockSpec(memory_space=pltpu.HBM)] * len(args),
             out_specs=(
-                pl.BlockSpec(memory_space=pltpu.VMEM),
                 pl.BlockSpec(memory_space=pltpu.VMEM),
                 pl.BlockSpec(memory_space=pltpu.VMEM),
             ),
@@ -430,26 +450,28 @@
                 pltpu.SMEM(orbitals.shape, jnp.int32),
                 pltpu.VMEM(coords.shape, jnp.float32),
                 pltpu.VMEM((2,) + reactant.shape, jnp.float32),
-                pltpu.VMEM(tiles[1:], jnp.float32),
-                pltpu.VMEM(tiles[1:], jnp.float32),
-                pltpu.VMEM(tiles[1:], jnp.float32),
                 pltpu.VMEM(tiles, jnp.float32),
                 pltpu.VMEM(tiles, jnp.float32),
                 pltpu.VMEM(tiles, jnp.float32),
+                pltpu.VMEM((n_hi, n_lo) + tiles, jnp.float32),
+                pltpu.VMEM((n_hi, n_lo) + tiles, jnp.float32),
+                pltpu.VMEM((n_lo, n_hi) + tiles, jnp.float32),
+                pltpu.VMEM((n_hi,) + tiles, jnp.float32),
+                pltpu.VMEM((n_hi,) + tiles, jnp.float32),
                 dma((n_slots // chunk, 4)),
                 dma((9,)),
                 dma((2,)),
                 dma((2,)),
-                dma((n_atom,)),
-                dma((n_atom,)),
-                dma((n_atom,)),
-                dma((n_atom,)),
+                dma((2, n_hi)),
+                dma((2, n_hi)),
+                dma((2, n_hi)),
+                dma((2, n_hi)),
             ],
             compiler_params=pltpu.CompilerParams(
                 collective_id=0, has_side_effects=True, vmem_limit_bytes=63 * 1024 * 1024
             ),
         )(*args)
-        return jnp.transpose(force + pull, (1, 0, 2)), jnp.reshape(along, (1,))
+        return jnp.transpose(band, (1, 0, 2)), jnp.reshape(along, (1,))
 
     return jax.shard_map(
         local,

time: 24.8 us -> 28.5 us (1.15)
  Pallas kernels: 20.1 us -> 23.8 us
  other arithmetic: 1.31 us -> 0 us
  local copies, waits for them, and re-layouts: 0 us -> 1.29 us
    pallas_call x1, Pallas kernels: 20.1 us -> 23.8 us  [local(): pl.pallas_call(functools.partial(step_kernel, n_img, n_atom, chunk), out_...]
    transpose x1 -> x0, other arithmetic: 1.31 us -> none  [local(): return (jnp.transpose(force + pull, (1, 0, 2)), jnp.reshape(along, (1,)))]
    unnamed x0 -> x1, local copies, waits for them, and re-layouts: none -> 1.29 us
where the time goes in v3:
time: 28.5 us; the launch traced here: 28.2 us
  Pallas kernels  23.8 us (84%)
  between operations  3.05 us (11%)
  local copies, waits for them, and re-layouts  1.29 us (5%)
    pallas_call x1, Pallas kernels, local(): pl.pallas_call(functools.partial(step_kernel, n_img, n_atom, chunk), out_...  23.8 us
    unnamed x1, local copies, waits for them, and re-layouts  1.29 us

profile of v3, /device:TPU:0, one launch (start us, length us, event | category | flops | bytes accessed | tf_op | source)
XLA Modules:
  0.0 28.2 jit_solution(12650489618951975769)
XLA Ops:
  1.3 23.8 %shard_map.140 = (f32[3,1,512]{2,1,0:T(1,128)}, f32[1,1]{1,0:T(1,128)}) custom-call(bf16[1,9,9,3072]{3,2,1,0:T(8,128)(2,1)} %density.1, bf16[1,9,9,3072]{3,2,1,0:T(8,128)(2,1)} %energy.1, bf16[1,9,9,3,3072]{4,3,2,1,0:T(4,128)(2,1)} %bitcast.5, bf16[1,9,9,3,3072]{4,3,2,1,0:T(4,128)(2,1)} %bitcast.6, s32[1,3072]{1,0:T(1,128)} %owner.1, s32[1,3072]{1,0:T(1,128)} %partner.1, ...), custom_call_target="tpu_custom_call" | custom-call | tf_op jit(solution)/shard_map/pallas_call | solution.py:422
  25.1 1.3 %copy.18 = f32[1,3,512]{2,0,1:T(1,128)} copy(f32[1,3,512]{2,0,1:T(1,128)} %bitcast.7) | data formatting | bytes 12288

commit v4 on v2

--- a/solution.py
+++ b/solution.py
@@ -31,8 +31,7 @@
     coords,
     reactant,
     product,
-    force_out,
-    pull_out,
+    band_out,
     tangent_out,
     dens_v,
     ener_v,
@@ -78,14 +77,28 @@
     tile = rows_own * LINES
     n_chunks = n_slots // chunk
 
+    barrier = pltpu.get_barrier_semaphore()
+    for s in range(1, n_atom):
+        pl.semaphore_signal(
+            barrier, inc=1, device_id={"atom": lax.rem(me + s, n_atom)}, device_id_type=MESH
+        )
+
+    @pl.when(img > 0)
+    def _():
+        pl.semaphore_signal(barrier, inc=1, device_id={"img": img - 1}, device_id_type=MESH)
+
+    @pl.when(img < n_img - 1)
+    def _():
+        pl.semaphore_signal(barrier, inc=1, device_id={"img": img + 1}, device_id_type=MESH)
+
     smalls = [
+        (coords, coords_v),
         (owner, owner_v),
         (partner, partner_v),
         (partner_species, kind_v),
         (count, count_s),
         (species, species_v),
         (orbitals, orbitals_s),
-        (coords, coords_v),
     ]
     small_copies = [
         pltpu.make_async_copy(src, dst, small_sem.at[i]) for i, (src, dst) in enumerate(smalls)
@@ -116,21 +129,7 @@
 
     lax.fori_loop(0, n_chunks, fetch, 0)
 
-    barrier = pltpu.get_barrier_semaphore()
-    for s in range(1, n_atom):
-        pl.semaphore_signal(
-            barrier, inc=1, device_id={"atom": lax.rem(me + s, n_atom)}, device_id_type=MESH
-        )
-
-    @pl.when(img > 0)
-    def _():
-        pl.semaphore_signal(barrier, inc=1, device_id={"img": img - 1}, device_id_type=MESH)
-
-    @pl.when(img < n_img - 1)
-    def _():
-        pl.semaphore_signal(barrier, inc=1, device_id={"img": img + 1}, device_id_type=MESH)
-
-    for copy in small_copies:
+    for copy in small_copies[1:]:
         copy.wait()
 
     kinds_own = species_v[...].reshape(1, species.shape[0])
@@ -183,7 +182,6 @@
         return carry
 
     def work(k, carry):
-        pl.when(k == middle)(send_tangent)
         cols = columns(k)
         own_orb, part_orb = orb_v[0:1, cols], orb_v[1:2, cols]
         for j, (src, dst) in enumerate(block_pairs(k)):
@@ -301,6 +299,7 @@
     greeted = (n_atom - 1) + jnp.where(img > 0, 1, 0) + jnp.where(img < n_img - 1, 1, 0)
 
     def send_coords():
+        small_copies[0].wait()
         to_tile(current_t, lambda c: coords_v[c])
         pl.semaphore_wait(barrier, greeted)
         pl.when(img < n_img - 1)(lambda: to_next().start())
@@ -329,11 +328,11 @@
         for s in range(1, n_atom):
             tangent_copy(s).start()
 
-    middle = min(2, n_chunks - 1)
     total[...] = jnp.zeros_like(total)
     total_own[...] = jnp.zeros_like(total_own)
+    send_coords()
     lax.fori_loop(0, n_chunks, prepare, 0)
-    send_coords()
+    send_tangent()
     lax.fori_loop(0, n_chunks, work, 0)
 
     for s in range(1, n_atom):
@@ -369,12 +368,11 @@
     for d in range(1, n_atom):
         summed = summed + recv_all[d]
     along = jnp.sum(summed[LINES - 1 : LINES], keepdims=True) * inverse
-    pull = ((spring - along) * inverse) * tan_all[me]
+    band = summed + ((spring - along) * inverse) * tan_all[me]
     for h in range(rows_own):
         for c in range(n_comp):
             row = h * LINES + c
-            force_out[c, :, h * WIDE : (h + 1) * WIDE] = summed[row : row + 1]
-            pull_out[c, :, h * WIDE : (h + 1) * WIDE] = pull[row : row + 1]
+            band_out[c, :, h * WIDE : (h + 1) * WIDE] = band[row : row + 1]
     tangent_out[...] = along
     pl.when(img < n_img - 1)(lambda: to_next().wait_send())
     pl.when(img > 0)(lambda: to_previous().wait_send())
@@ -397,16 +395,14 @@
         tile = species.shape[0] // WIDE * LINES
         tiles = (n_atom, tile, WIDE)
         dma = pltpu.SemaphoreType.DMA
-        force, pull, along = pl.pallas_call(
+        band, along = pl.pallas_call(
             functools.partial(step_kernel, n_img, n_atom, chunk),
             out_shape=(
-                jax.ShapeDtypeStruct(coords.shape, jnp.float32),
                 jax.ShapeDtypeStruct(coords.shape, jnp.float32),
                 jax.ShapeDtypeStruct((1, 1), jnp.float32),
             ),
             in_specs=[pl.BlockSpec(memory_space=pltpu.HBM)] * len(args),
             out_specs=(
-                pl.BlockSpec(memory_space=pltpu.VMEM),
                 pl.BlockSpec(memory_space=pltpu.VMEM),
                 pl.BlockSpec(memory_space=pltpu.VMEM),
             ),
@@ -449,7 +445,7 @@
                 collective_id=0, has_side_effects=True, vmem_limit_bytes=63 * 1024 * 1024
             ),
         )(*args)
-        return jnp.transpose(force + pull, (1, 0, 2)), jnp.reshape(along, (1,))
+        return jnp.transpose(band, (1, 0, 2)), jnp.reshape(along, (1,))
 
     return jax.shard_map(
         local,

time: 24.8 us -> 24.5 us (0.988)
  other arithmetic: 1.31 us -> 0 us
  local copies, waits for them, and re-layouts: 0 us -> 1.29 us
    transpose x1 -> x0, other arithmetic: 1.31 us -> none  [local(): return (jnp.transpose(force + pull, (1, 0, 2)), jnp.reshape(along, (1,)))]
    unnamed x0 -> x1, local copies, waits for them, and re-layouts: none -> 1.29 us
where the time goes in v4:
time: 24.5 us; the launch traced here: 24.3 us
  Pallas kernels  19.9 us (81%)
  between operations  3.05 us (12%)
  local copies, waits for them, and re-layouts  1.29 us (5%)
    pallas_call x1, Pallas kernels, local(): pl.pallas_call(functools.partial(step_kernel, n_img, n_atom, chunk), out_...  19.9 us
    unnamed x1, local copies, waits for them, and re-layouts  1.29 us

profile of v4, /device:TPU:0, one launch (start us, length us, event | category | flops | bytes accessed | tf_op | source)
XLA Modules:
  0.0 24.3 jit_solution(4748308188111274022)
XLA Ops:
  1.3 19.9 %shard_map.140 = (f32[3,1,512]{2,1,0:T(1,128)}, f32[1,1]{1,0:T(1,128)}) custom-call(bf16[1,9,9,3072]{3,2,1,0:T(8,128)(2,1)} %density.1, bf16[1,9,9,3072]{3,2,1,0:T(8,128)(2,1)} %energy.1, bf16[1,9,9,3,3072]{4,3,2,1,0:T(4,128)(2,1)} %bitcast.5, bf16[1,9,9,3,3072]{4,3,2,1,0:T(4,128)(2,1)} %bitcast.6, s32[1,3072]{1,0:T(1,128)} %owner.1, s32[1,3072]{1,0:T(1,128)} %partner.1, ...), custom_call_target="tpu_custom_call" | custom-call | tf_op jit(solution)/shard_map/pallas_call | solution.py:398
  21.2 1.3 %copy.18 = f32[1,3,512]{2,0,1:T(1,128)} copy(f32[1,3,512]{2,0,1:T(1,128)} %bitcast.7) | data formatting | bytes 12288
